TPU v7x, 32 devices: a whole 2x2x4 slice. The times are simulated.
32 devices in a mesh: grp: 8 (over y, x, core), seq: 4 (over z).
Axes of the slice: x: 2, y: 2, z: 4, core: 2. Of those that a mesh axis runs over, the one named last changes fastest.
Arguments:
- prompt_hidden: bfloat16 [8, 4096, 5120], P('grp', 'seq'), may hold values from -6 to 6
- resp_hidden: bfloat16 [8, 512, 5120], P('grp', 'seq'), may hold values from -6 to 6
- queries: bfloat16 [8, 512, 1024], P('grp', 'seq'), may hold values from -180 to 180
- grad_out: bfloat16 [8, 512, 1024], P('grp', 'seq'), may hold values from -6 to 6
- kv_weight: bfloat16 [5120, 256], P(('grp', 'seq')), may hold values from -0.078125 to 0.078125
- prompt_lengths: int32 [8], P('grp'), may hold values from 2048 to 4096
- response_lengths: int32 [8, 4], P('grp'), may hold values from 1 to 128, 320 in all within a row
Outputs:
- attended: bfloat16 [8, 512, 1024], P('grp', 'seq')
- query_grad: bfloat16 [8, 512, 1024], P('grp', 'seq')
- prompt_kv_grad: bfloat16 [8, 4096, 256], P('grp', 'seq')
- weight_grad: float32 [5120, 256], P(('grp', 'seq'))
Inputs may be any that keep to these rules, and one draw needn't show every extreme that they name: `response_lengths`: every prompt has one response of exactly 128 live tokens.
All inputs are finite; a program needn't handle non-finite values.
Results may differ from a plain program's by a relative error of at most 0.025.
The roundings to bfloat16 on the way count: a program that leaves them out, or rounds other values in their place, can miss the bound.
Values may be sent and summed in bfloat16 or wider, within the bound.
A program may use at most 128 MiB of HBM per device.

v0:
```python
import jax
import jax.numpy as jnp
from jax import lax
from jax.sharding import PartitionSpec as P


def per_device(
    prompt_hidden, resp_hidden, queries, grad_out, kv_weight, prompt_lengths, response_lengths
):
    seq_rank = lax.axis_index("seq")
    head_dim = kv_weight.shape[1] // 2
    rt_dev = resp_hidden.shape[1]
    width = queries.shape[2]
    heads = width // head_dim
    group_heads = 2
    blocks = heads // group_heads
    scale = head_dim ** (-0.5)
    prompt_rows = prompt_hidden[0]
    resp_rows = resp_hidden[0]
    piece = lax.all_gather(kv_weight, ("grp", "seq"), axis=0, tiled=True)
    left = prompt_rows
    right = resp_rows
    own_kv = jnp.dot(left, piece, preferred_element_type=jnp.float32)
    resp_kv = jnp.dot(right, piece, preferred_element_type=jnp.float32)
    own_kv = own_kv.astype(jnp.bfloat16)
    resp_kv = resp_kv.astype(jnp.bfloat16)
    prompt_kv = lax.all_gather(own_kv, "seq", axis=0, tiled=True)
    plen_all = prompt_kv.shape[0]
    prompt_len = prompt_lengths[0]
    lengths_row = response_lengths[0]
    members = jnp.arange(lengths_row.shape[0])
    resp_len = jnp.sum(jnp.where(members == seq_rank, lengths_row, 0))
    position = jnp.arange(rt_dev)
    live = position < resp_len
    prompt_ok = jnp.arange(plen_all) < prompt_len
    allowed = jnp.concatenate(
        [
            jnp.broadcast_to(prompt_ok[None, :], (rt_dev, plen_all)),
            position[None, :] <= position[:, None],
        ],
        1,
    )
    keys = jnp.concatenate([prompt_kv[:, :head_dim], resp_kv[:, :head_dim]], 0)
    values = jnp.concatenate([prompt_kv[:, head_dim:], resp_kv[:, head_dim:]], 0)
    grad_live = jnp.where(live[:, None], grad_out[0], jnp.zeros_like(grad_out[0]))
    q_blocks = queries[0].reshape(rt_dev, blocks, group_heads, head_dim).transpose(1, 0, 2, 3)
    g_blocks = grad_live.reshape(rt_dev, blocks, group_heads, head_dim).transpose(1, 0, 2, 3)

    def attend_block(pieces):
        q_part, g_part = pieces
        scores = jnp.einsum("thd,kd->htk", q_part, keys, preferred_element_type=jnp.float32) * scale
        scores = jnp.where(allowed[None], scores, -jnp.inf)
        top = jnp.max(scores, 2, keepdims=True)
        expo = jnp.exp(scores - top)
        total = jnp.sum(expo, 2, keepdims=True)
        probs = expo / total
        probs_b = probs.astype(jnp.bfloat16)
        out_part = jnp.einsum("htk,kd->thd", probs_b, values, preferred_element_type=jnp.float32)
        out_part = jnp.where(live[:, None, None], out_part, jnp.zeros_like(out_part)).astype(
            jnp.bfloat16
        )
        delta = jnp.sum(g_part.astype(jnp.float32) * out_part.astype(jnp.float32), 2).T
        dprob = jnp.einsum("thd,kd->htk", g_part, values, preferred_element_type=jnp.float32)
        dscore = (probs * (dprob - delta[:, :, None]) * scale).astype(jnp.bfloat16)
        q_grad = jnp.einsum("htk,kd->thd", dscore, keys, preferred_element_type=jnp.float32).astype(
            jnp.bfloat16
        )
        key_grad = jnp.einsum("htk,thd->kd", dscore, q_part, preferred_element_type=jnp.float32)
        value_grad = jnp.einsum("htk,thd->kd", probs_b, g_part, preferred_element_type=jnp.float32)
        return (out_part, q_grad, key_grad, value_grad, top[:, :, 0], total[:, :, 0], delta)

    out_b, qg_b, key_grad, value_grad, tops, totals, deltas = lax.map(
        attend_block, (q_blocks, g_blocks)
    )
    attended = out_b.transpose(1, 0, 2, 3).reshape(rt_dev, width)
    query_grad = qg_b.transpose(1, 0, 2, 3).reshape(rt_dev, width)
    kv_grad = jnp.concatenate([jnp.sum(key_grad, 0), jnp.sum(value_grad, 0)], 1)
    resp_grad = kv_grad[plen_all:]
    prompt_grad = lax.psum_scatter(
        kv_grad[None, :plen_all], "seq", scatter_dimension=1, tiled=True
    )[0]
    prompt_grad = prompt_grad.astype(jnp.bfloat16)
    resp_grad = resp_grad.astype(jnp.bfloat16)
    contract = (((0,), (0,)), ((), ()))
    left = prompt_rows
    right = resp_rows
    term = lax.dot_general(left, prompt_grad, contract, preferred_element_type=jnp.float32)
    weight_grad = lax.psum_scatter(
        term + lax.dot_general(right, resp_grad, contract, preferred_element_type=jnp.float32),
        ("grp", "seq"),
        scatter_dimension=0,
        tiled=True,
    )
    return (attended[None], query_grad[None], prompt_grad[None], weight_grad)


def solution(mesh):
    return jax.shard_map(
        per_device,
        mesh=mesh,
        in_specs=(
            P("grp", "seq", None),
            P("grp", "seq", None),
            P("grp", "seq", None),
            P("grp", "seq", None),
            P(("grp", "seq"), None),
            P("grp"),
            P("grp", None),
        ),
        out_specs=(
            P("grp", "seq", None),
            P("grp", "seq", None),
            P("grp", "seq", None),
            P(("grp", "seq"), None),
        ),
        check_vma=False,
    )
```

profile of v0, /device:TPU:0, one launch (start us, length us, event | category | flops | bytes accessed | tf_op | source)
XLA Modules:
  0.0 446.8 jit_solution(13525319538324743184)
XLA Ops:
  7.2 0.7 all-gather.3.cloned.1.call-update
  8.0 63.7 %all-gather.3.cloned.1.call-done = bf16[5120,256]{1,0:T(8,128)(2,1)} async-done(((bf16[160,256]{1,0:T(8,128)(2,1)}), bf16[5120,256]{1,0:T(8,128)(2,1)}) %all-gather.3.cloned.1.call-update) | async-done | bytes 2621456 | tf_op jit(solution)/shard_map/all_gather | solution.py:20
  71.7 8.4 %fusion.43 = bf16[1024,256]{1,0:T(8,128)(2,1)} fusion(bf16[5120,256]{1,0:T(8,128)(2,1)} %all-gather.3.cloned.1.call-done, bf16[1,1024,5120]{2,1,0:T(8,128)(2,1)} %param.9), kind=kOutput, calls=%fused_computation.56 | convolution fusion | flops 2684616704 | bytes 13631488 | tf_op jit(solution)/shard_map/dot_general | solution.py:23
  80.8 0.8 copy.38
  81.7 0.2 copy.39
  81.9 0.6 fusion.52
  82.5 0.6 iota_compare_fusion.3
  83.1 0.7 select_bitcast_fusion
  83.9 1.0 pad_add_fusion
  84.8 2.4 fusion.46
  87.2 37.9 %all-gather.5.cloned.1.call-done = bf16[4096,256]{1,0:T(8,128)(2,1)} async-done(((bf16[1024,256]{1,0:T(8,128)(2,1)}), bf16[4096,256]{1,0:T(8,128)(2,1)}) %all-gather.5.cloned.1.call-update) | async-done | bytes 2097168 | tf_op jit(solution)/shard_map/all_gather | solution.py:27
  125.1 1.7 fusion.55
  126.8 0.1 pad_maximum_fusion
  126.9 52.6 %while.17 = (s32[]{:T(128)}, bf16[4,128,2,128]{1,3,2,0:T(8,128)(2,1)}, bf16[4,128,2,128]{3,1,2,0:T(8,128)(2,1)}, f32[4,4224,128]{2,1,0:T(8,128)}, f32[4,4224,128...) while((s32[]{:T(128)}, ...), condition=%wide.region_5.6_spmd.clone, body=%wide.region_1.5_spmd.clone.sunk | while | flops 1673072640 | bytes 45440432 | solution.py:72
  126.9 0.6 iota_compare_fusion.5
  127.5 1.9 fusion.95
  129.5 1.1 fusion.96
  130.6 0.3 fusion.97
  130.9 1.5 bitcast_dynamic-update-slice_fusion.2
  132.5 1.1 fusion.98
  133.6 1.4 fusion.99
  135.0 3.0 fusion.100
  138.0 2.2 fusion.101
  140.2 0.6 iota_compare_fusion.5
  140.8 1.9 fusion.95
  142.7 1.1 fusion.96
  143.8 0.3 fusion.97
  144.2 1.5 bitcast_dynamic-update-slice_fusion.2
  145.7 1.1 fusion.98
  146.9 1.4 fusion.99
  148.2 3.0 fusion.100
  151.2 2.1 fusion.101
  153.3 0.6 iota_compare_fusion.5
  153.9 1.9 fusion.95
  155.8 1.1 fusion.96
  157.0 0.3 fusion.97
  157.3 1.5 bitcast_dynamic-update-slice_fusion.2
  158.9 1.1 fusion.98
  160.0 1.4 fusion.99
  161.3 3.0 fusion.100
  164.3 2.1 fusion.101
  166.4 0.6 iota_compare_fusion.5
  167.0 1.9 fusion.95
  169.0 1.1 fusion.96
  170.1 0.3 fusion.97
  170.4 1.5 bitcast_dynamic-update-slice_fusion.2
  172.0 1.1 fusion.98
  173.1 1.3 fusion.99
  174.5 3.0 fusion.100
  177.5 2.1 fusion.101
  179.6 4.2 reduce_sum.47
  183.7 5.6 %reduce_sum.46 = f32[4224,128]{1,0:T(8,128)} reduce(f32[4,4224,128]{2,1,0:T(8,128)} %get-tuple-element.66, f32[]{:T(128)} %constant.23.clone.1), dimensions={0}, to_apply=%region_6.7 | reduce | flops 1622016 | bytes 10813444 | tf_op jit(solution)/shard_map/reduce_sum | solution.py:77
  189.3 3.8 fusion.39
  193.1 0.2 reduce-scatter.7.cloned.1.call-start
  193.4 75.4 %reduce-scatter.5.cloned.1.call-done = f32[1,1024,256]{2,1,0:T(8,128)} async-done(((f32[1,4096,256]{2,1,0:T(8,128)}), f32[1,1024,256]{2,1,0:T(8,128)}) %reduce-scatter.5.cloned.1.call-update) | async-done | bytes 1048592 | tf_op jit(solution)/shard_map/reduce_scatter | solution.py:79
  268.8 1.3 convert_element_type.40
  270.1 5.8 %fusion.33 = f32[256,5120]{1,0:T(8,128)S(1)} fusion(bf16[1,1024,5120]{2,1,0:T(8,128)(2,1)} %param.9, bf16[1,1024,256]{2,1,0:T(8,128)(2,1)S(1)} %convert_element_type.40), kind=kOutput, calls=%fused_computation.42 | convolution fusion | flops 2684354560 | bytes 16252928 | tf_op jit(solution)/shard_map/dot_general | solution.py:87
  275.9 3.2 fusion.37
  279.1 5.9 %copy.52 = f32[5120,256]{1,0:T(8,128)} copy(f32[5120,256]{0,1:T(8,128)} %fusion.37) | data formatting | bytes 10485760
  285.1 0.9 copy-done.7
  286.0 0.8 copy.50
  286.8 0.3 copy.43
  287.1 0.9 broadcast_in_dim_reshape.7
  288.0 152.3 %reduce-scatter.7.cloned.1.call-done = f32[160,256]{1,0:T(8,128)} async-done(((f32[5120,256]{1,0:T(8,128)}), f32[160,256]{1,0:T(8,128)}) %reduce-scatter.7.cloned.1.call-update) | async-done | bytes 163856
  (41 shorter events, 0.4 us)
Async XLA Ops:
  7.2 77.6 %copy-start = (bf16[1,128,5120]{2,1,0:T(8,128)(2,1)S(1)}, bf16[1,128,5120]{2,1,0:T(8,128)(2,1)}, u32[]{:S(2)}) copy-start(bf16[1,128,5120]{2,1,0:T(8,128)(2,1)} %param.10) | copy-start | bytes 3932164
  7.2 64.5 %all-gather.3.cloned.1.call-start = ((), (), s32[]{:S(2)}) async-start(), calls=%async_computation.2 | async-start | bytes 2703360 | tf_op jit(solution)/shard_map/all_gather | solution.py:20
  7.9 72.9 %copy-start.4 = (bf16[1,128,1024]{2,1,0:T(8,128)(2,1)S(1)}, bf16[1,128,1024]{2,1,0:T(8,128)(2,1)}, u32[]{:S(2)}) copy-start(bf16[1,128,1024]{2,1,0:T(8,128)(2,1)} %param.11) | copy-start | bytes 786436
  7.9 73.8 %copy-start.5 = (bf16[1,128,1024]{2,1,0:T(8,128)(2,1)S(1)}, bf16[1,128,1024]{2,1,0:T(8,128)(2,1)}, u32[]{:S(2)}) copy-start(bf16[1,128,1024]{2,1,0:T(8,128)(2,1)} %param.12) | copy-start | bytes 786436
  7.9 74.0 %copy-start.8 = (s32[1,4]{1,0:T(1,128)S(1)}, s32[1,4]{1,0:T(1,128)}, u32[]{:S(2)}) copy-start(s32[1,4]{1,0:T(1,128)} %param.15) | copy-start | bytes 52
  7.9 117.2 %all-gather.5.cloned.1.call-start = ((), (), s32[]{:S(2)}) async-start(), calls=%async_computation.3 | async-start | bytes 2621440 | tf_op jit(solution)/shard_map/all_gather | solution.py:27
  80.1 188.7 %reduce-scatter.5.cloned.1.call-start = ((), (), s32[]{:S(2)}) async-start(), calls=%async_computation.4 | async-start | bytes 5242880 | tf_op jit(solution)/shard_map/reduce_scatter | solution.py:79
  130.9 1.5 copy-start.2
  144.2 1.5 copy-start.2
  157.3 1.5 copy-start.2
  170.4 1.5 copy-start.2
  193.1 247.1 %reduce-scatter.7.cloned.1.call-start = ((), (), s32[]{:S(2)}) async-start(), calls=%async_computation.5 | async-start | bytes 5406720
  270.1 5.9 %copy-start.3 = (bf16[1,1024,256]{2,1,0:T(8,128)(2,1)}, bf16[1,1024,256]{2,1,0:T(8,128)(2,1)S(1)}, u32[]{:S(2)}) copy-start(bf16[1,1024,256]{2,1,0:T(8,128)(2,1)S(1)} %convert_element_type.40) | copy-start | bytes 1572868
  270.1 5.9 %copy-start.1 = (f32[4224,128]{1,0:T(8,128)S(1)}, f32[4224,128]{1,0:T(8,128)}, u32[]{:S(2)}) copy-start(f32[4224,128]{1,0:T(8,128)} %reduce_sum.46) | copy-start | bytes 6488068
  285.0 0.9 copy-start.7
  285.0 1.8 copy-start.6
Sparse Core Ops, SparseCore 0:
  10.9 60.7 all-gather.2
  80.2 44.8 all-gather.4
  193.3 75.4 reduce-scatter.4
  285.2 155.0 reduce-scatter.6
where the time goes:
time: 448 us; the launch traced here: 447 us
  waiting for transfers between devices  330 us (74%)
  matrix products  64 us (14%)
  other arithmetic  26.1 us (6%)
  between operations  14.6 us (3%)
  local copies, waits for them, and re-layouts  11.6 us (3%)
    unnamed x5, waiting for transfers between devices  153 us
    reduce_scatter x1, waiting for transfers between devices, per_device(): lax.psum_scatter(kv_grad[None, :plen_all], 'seq', scatter_dimension=1, ti...  75.4 us
    all_gather x1, waiting for transfers between devices, per_device(): piece = lax.all_gather(kv_weight, ('grp', 'seq'), axis=0, tiled=True)  63.7 us
    all_gather x1, waiting for transfers between devices, per_device(): prompt_kv = lax.all_gather(own_kv, 'seq', axis=0, tiled=True)  37.9 us
    dot_general x4, matrix products, attend_block(): jnp.einsum('htk,thd->kd', dscore, q_part, preferred_element_type=jnp.floa...  11.9 us
    reduce_sum x2, other arithmetic, per_device(): kv_grad = jnp.concatenate([jnp.sum(key_grad, 0), jnp.sum(value_grad, 0)], 1)  9.74 us
  transfers between devices with their start and end apart: 4, of which 4 were waited for; matrix products, arithmetic and copies ran while one was open for 2% of the time, Pallas kernels for 0%

commit v1 on v0

--- a/solution.py
+++ b/solution.py
@@ -1,10 +1,244 @@
+import functools
+
 import jax
 import jax.numpy as jnp
 from jax import lax
+from jax.experimental import pallas as pl
+from jax.experimental.pallas import tpu as pltpu
 from jax.sharding import PartitionSpec as P
 
+MESH = pl.DeviceIdType.MESH
+CORES = 2
+
+
+def place(cols):
+    grp = lax.axis_index("grp")
+    seq = lax.axis_index("seq")
+    return grp, seq, grp // CORES, grp % CORES
+
+
+def greet(cols, seqs):
+    grp, seq, col, core = place(cols)
+    barrier = pltpu.get_barrier_semaphore()
+    peers = [(grp, (seq + k) % seqs) for k in range(1, seqs)]
+    peers += [(((col + j) % cols) * CORES + core, seq) for j in range(1, cols)]
+    peers += [(col * CORES + 1 - core, seq)]
+    for peer in peers:
+        pl.semaphore_signal(barrier, inc=1, device_id=peer, device_id_type=MESH)
+    pl.semaphore_wait(barrier, len(peers))
+
+
+def remote(src, dst, send, recv, device):
+    return pltpu.make_async_remote_copy(
+        src_ref=src, dst_ref=dst, send_sem=send, recv_sem=recv, device_id=device, device_id_type=MESH
+    )
+
+
+def gather_kernel(cols, seqs, w_ref, out_ref, zs, zr, xs, xr, cs, cr, own_sem):
+    grp, seq, col, core = place(cols)
+    sibling = (col * CORES + 1 - core, seq)
+    greet(cols, seqs)
+    own = pltpu.make_async_copy(w_ref.at[0], out_ref.at[grp * seqs + seq], own_sem)
+    own.start()
+    sent = []
+    for k in range(1, seqs):
+        copy = remote(
+            w_ref.at[0], out_ref.at[grp * seqs + seq], zs.at[k - 1], zr.at[k - 1], (grp, (seq + k) % seqs)
+        )
+        copy.start()
+        sent.append(copy)
+    first = list(sent)
+    across = {}
+    over = []
+    for k in range(seqs):
+        if k:
+            first[k - 1].wait_recv()
+        index = grp * seqs + (seq + seqs - k) % seqs
+        src = w_ref.at[0] if k == 0 else out_ref.at[index]
+        for j in range(1, cols):
+            copy = remote(
+                src, out_ref.at[index], xs.at[k, j - 1], xr.at[k, j - 1], (((col + j) % cols) * CORES + core, seq)
+            )
+            copy.start()
+            across[k, j] = copy
+        copy = remote(src, out_ref.at[index], cs.at[k, 0], cr.at[k, 0], sibling)
+        copy.start()
+        over.append(copy)
+    for k in range(seqs):
+        for j in range(1, cols):
+            across[k, j].wait_recv()
+            index = (((col + cols - j) % cols) * CORES + core) * seqs + (seq + seqs - k) % seqs
+            copy = remote(out_ref.at[index], out_ref.at[index], cs.at[k, j], cr.at[k, j], sibling)
+            copy.start()
+            over.append(copy)
+    for copy in over:
+        copy.wait_recv()
+    for copy in sent + list(across.values()) + over:
+        copy.wait_send()
+    own.wait()
+
+
+def gather_weight(weight, cols, seqs):
+    rows, width = weight.shape
+    out = pl.pallas_call(
+        functools.partial(gather_kernel, cols, seqs),
+        out_shape=jax.ShapeDtypeStruct((cols * CORES * seqs, rows, width), weight.dtype),
+        in_specs=[pl.BlockSpec(memory_space=pl.ANY)],
+        out_specs=pl.BlockSpec(memory_space=pl.ANY),
+        scratch_shapes=[
+            pltpu.SemaphoreType.DMA((seqs - 1,)),
+            pltpu.SemaphoreType.DMA((seqs - 1,)),
+            pltpu.SemaphoreType.DMA((seqs, cols - 1)),
+            pltpu.SemaphoreType.DMA((seqs, cols - 1)),
+            pltpu.SemaphoreType.DMA((seqs, cols)),
+            pltpu.SemaphoreType.DMA((seqs, cols)),
+            pltpu.SemaphoreType.DMA,
+        ],
+        compiler_params=pltpu.CompilerParams(collective_id=0, has_side_effects=True),
+        name="gather_weight",
+    )(weight[None])
+    return out.reshape(cols * CORES * seqs * rows, width)
+
+
+def finish_kernel(
+    cols, seqs, part_ref, rgrad_ref, x_ref, xr_ref, pgrad_ref, wgrad_ref,
+    xbuf, gt, ksend, krecv, pair, crecv, xsend, xrecv, total, zsend, zrecv,
+    xsem, ks, kr, cs, cr, xs, xr, zs, zr,
+):
+    grp, seq, col, core = place(cols)
+    sibling = (col * CORES + 1 - core, seq)
+    plen, width = pgrad_ref.shape
+    rt = rgrad_ref.shape[0]
+    block = pair.shape[1]
+    half = block // CORES
+    rows = wgrad_ref.shape[0]
+    loads = []
+    for j in range(cols):
+        at = pl.ds(pl.multiple_of(((col + j) % cols) * block, 128), block)
+        loads.append(pltpu.make_async_copy(x_ref.at[:, at], xbuf.at[j, pl.ds(0, plen)], xsem.at[0, j]))
+        loads.append(pltpu.make_async_copy(xr_ref.at[:, at], xbuf.at[j, pl.ds(plen, rt)], xsem.at[1, j]))
+    for load in loads:
+        load.start()
+    greet(cols, seqs)
+
+    sends = []
+    for k in range(1, seqs):
+        ksend[k - 1] = part_ref[(seq + k) % seqs].astype(jnp.bfloat16)
+        copy = remote(
+            ksend.at[k - 1], krecv.at[k - 1], ks.at[k - 1], kr.at[k - 1], (grp, (seq + k) % seqs)
+        )
+        copy.start()
+        sends.append(copy)
+    gt[:, pl.ds(plen, rt)] = rgrad_ref[...].astype(jnp.float32).T.astype(jnp.bfloat16)
+    for load in loads:
+        load.wait()
+    for copy in sends:
+        copy.wait_recv()
+    for t in range(0, plen, 256):
+        at = pl.ds(t, 256)
+        acc = part_ref[seq, at, :]
+        for k in range(1, seqs):
+            acc = acc + krecv[k - 1, at, :].astype(jnp.float32)
+        grad = acc.astype(jnp.bfloat16)
+        pgrad_ref[at, :] = grad
+        gt[:, at] = grad.astype(jnp.float32).T.astype(jnp.bfloat16)
+
+    tile = 256 if block % 256 == 0 else 128
+    mine = pl.ds(pl.multiple_of(core * half, 8), half)
+    other = pl.ds(pl.multiple_of((1 - core) * half, 8), half)
+    order = list(range(1, cols)) + [0]
+    over, across = {}, {}
+
+    def forward(j):
+        over[j].wait_recv()
+        xsend[j - 1] = (pair[j, mine, :] + crecv[j]).astype(jnp.bfloat16)
+        copy = remote(
+            xsend.at[j - 1], xrecv.at[j - 1], xs.at[j - 1], xr.at[j - 1],
+            (((col + j) % cols) * CORES + core, seq),
+        )
+        copy.start()
+        across[j] = copy
+
+    for step, j in enumerate(order):
+        for t in range(0, block, tile):
+            at = pl.ds(t, tile)
+            prod = jnp.dot(gt[...], xbuf[j, :, at], preferred_element_type=jnp.float32)
+            pair[j, at, :] = prod.T
+        copy = remote(pair.at[j, other], crecv.at[j], cs.at[j], cr.at[j], sibling)
+        copy.start()
+        over[j] = copy
+        if step:
+            forward(order[step - 1])
+    over[0].wait_recv()
+    total[...] = pair[0, mine, :] + crecv[0]
+    for j in range(1, cols):
+        across[j].wait_recv()
+        total[...] += xrecv[j - 1].astype(jnp.float32)
+
+    last = []
+    for k in range(1, seqs):
+        at = pl.ds(pl.multiple_of(((seq + k) % seqs) * rows, 8), rows)
+        zsend[k - 1] = total[at, :].astype(jnp.bfloat16)
+        copy = remote(
+            zsend.at[k - 1], zrecv.at[k - 1], zs.at[k - 1], zr.at[k - 1], (grp, (seq + k) % seqs)
+        )
+        copy.start()
+        last.append(copy)
+    acc = total[pl.ds(pl.multiple_of(seq * rows, 8), rows), :]
+    for k in range(1, seqs):
+        last[k - 1].wait_recv()
+        acc = acc + zrecv[k - 1].astype(jnp.float32)
+    wgrad_ref[...] = acc
+    for copy in sends + list(over.values()) + list(across.values()) + last:
+        copy.wait_send()
+
+
+def finish(part, rgrad, x, xr, cols, seqs):
+    plen, d = x.shape
+    rt = xr.shape[0]
+    width = part.shape[-1]
+    block = d // cols
+    half = block // CORES
+    rows = half // seqs
+    bf16, f32 = jnp.bfloat16, jnp.float32
+    vmem = pl.BlockSpec(memory_space=pltpu.VMEM)
+    hbm = pl.BlockSpec(memory_space=pl.ANY)
+    dma = pltpu.SemaphoreType.DMA
+    return pl.pallas_call(
+        functools.partial(finish_kernel, cols, seqs),
+        out_shape=(
+            jax.ShapeDtypeStruct((plen, width), bf16),
+            jax.ShapeDtypeStruct((rows, width), f32),
+        ),
+        in_specs=[vmem, vmem, hbm, hbm],
+        out_specs=(vmem, vmem),
+        scratch_shapes=[
+            pltpu.VMEM((cols, plen + rt, block), bf16),
+            pltpu.VMEM((width, plen + rt), bf16),
+            pltpu.VMEM((seqs - 1, plen, width), bf16),
+            pltpu.VMEM((seqs - 1, plen, width), bf16),
+            pltpu.VMEM((cols, block, width), f32),
+            pltpu.VMEM((cols, half, width), f32),
+            pltpu.VMEM((cols - 1, half, width), bf16),
+            pltpu.VMEM((cols - 1, half, width), bf16),
+            pltpu.VMEM((half, width), f32),
+            pltpu.VMEM((seqs - 1, rows, width), bf16),
+            pltpu.VMEM((seqs - 1, rows, width), bf16),
+            dma((2, cols)),
+            dma((seqs - 1,)), dma((seqs - 1,)),
+            dma((cols,)), dma((cols,)),
+            dma((cols - 1,)), dma((cols - 1,)),
+            dma((seqs - 1,)), dma((seqs - 1,)),
+        ],
+        compiler_params=pltpu.CompilerParams(
+            collective_id=1, has_side_effects=True, vmem_limit_bytes=52 * 2**20
+        ),
+        name="finish",
+    )(part, rgrad, x, xr)
+
 
 def per_device(
+    cols, seqs,
     prompt_hidden, resp_hidden, queries, grad_out, kv_weight, prompt_lengths, response_lengths
 ):
     seq_rank = lax.axis_index("seq")
@@ -17,11 +251,9 @@
     scale = head_dim ** (-0.5)
     prompt_rows = prompt_hidden[0]
     resp_rows = resp_hidden[0]
-    piece = lax.all_gather(kv_weight, ("grp", "seq"), axis=0, tiled=True)
-    left = prompt_rows
-    right = resp_rows
-    own_kv = jnp.dot(left, piece, preferred_element_type=jnp.float32)
-    resp_kv = jnp.dot(right, piece, preferred_element_type=jnp.float32)
+    piece = gather_weight(kv_weight, cols, seqs)
+    own_kv = jnp.dot(prompt_rows, piece, preferred_element_type=jnp.float32)
+    resp_kv = jnp.dot(resp_rows, piece, preferred_element_type=jnp.float32)
     own_kv = own_kv.astype(jnp.bfloat16)
     resp_kv = resp_kv.astype(jnp.bfloat16)
     prompt_kv = lax.all_gather(own_kv, "seq", axis=0, tiled=True)
@@ -67,36 +299,22 @@
         )
         key_grad = jnp.einsum("htk,thd->kd", dscore, q_part, preferred_element_type=jnp.float32)
         value_grad = jnp.einsum("htk,thd->kd", probs_b, g_part, preferred_element_type=jnp.float32)
-        return (out_part, q_grad, key_grad, value_grad, top[:, :, 0], total[:, :, 0], delta)
-
-    out_b, qg_b, key_grad, value_grad, tops, totals, deltas = lax.map(
-        attend_block, (q_blocks, g_blocks)
-    )
+        return (out_part, q_grad, key_grad, value_grad)
+
+    out_b, qg_b, key_grad, value_grad = lax.map(attend_block, (q_blocks, g_blocks))
     attended = out_b.transpose(1, 0, 2, 3).reshape(rt_dev, width)
     query_grad = qg_b.transpose(1, 0, 2, 3).reshape(rt_dev, width)
     kv_grad = jnp.concatenate([jnp.sum(key_grad, 0), jnp.sum(value_grad, 0)], 1)
-    resp_grad = kv_grad[plen_all:]
-    prompt_grad = lax.psum_scatter(
-        kv_grad[None, :plen_all], "seq", scatter_dimension=1, tiled=True
-    )[0]
-    prompt_grad = prompt_grad.astype(jnp.bfloat16)
-    resp_grad = resp_grad.astype(jnp.bfloat16)
-    contract = (((0,), (0,)), ((), ()))
-    left = prompt_rows
-    right = resp_rows
-    term = lax.dot_general(left, prompt_grad, contract, preferred_element_type=jnp.float32)
-    weight_grad = lax.psum_scatter(
-        term + lax.dot_general(right, resp_grad, contract, preferred_element_type=jnp.float32),
-        ("grp", "seq"),
-        scatter_dimension=0,
-        tiled=True,
-    )
+    resp_grad = kv_grad[plen_all:].astype(jnp.bfloat16)
+    part = kv_grad[:plen_all].reshape(seqs, plen_all // seqs, 2 * head_dim)
+    prompt_grad, weight_grad = finish(part, resp_grad, prompt_rows, resp_rows, cols, seqs)
     return (attended[None], query_grad[None], prompt_grad[None], weight_grad)
 
 
 def solution(mesh):
+    cols, seqs = mesh.shape["grp"] // CORES, mesh.shape["seq"]
     return jax.shard_map(
-        per_device,
+        functools.partial(per_device, cols, seqs),
         mesh=mesh,
         in_specs=(
             P("grp", "seq", None),

time: 448 us -> 231 us (0.52)
  waiting for transfers between devices: 330 us -> 39.6 us
  Pallas kernels: 0 us -> 100 us
  matrix products: 64 us -> 44.3 us
    unnamed x5 -> x1, waiting for transfers between devices: 153 us -> 0.02 us
    pallas_call x0 -> x2, Pallas kernels: none -> 100 us  [the longest x1 76.7 us: finish(): pl.pallas_call(functools.partial(finish_kernel, cols, seqs), out_shape=(j...]
    reduce_scatter x1 -> x0, waiting for transfers between devices: 75.4 us -> none  [per_device(): lax.psum_scatter(kv_grad[None, :plen_all], 'seq', scatter_dimension=1, ti...]
    all_gather x1 -> x0, waiting for transfers between devices: 63.7 us -> none  [per_device(): piece = lax.all_gather(kv_weight, ('grp', 'seq'), axis=0, tiled=True)]
    dot_general x4 -> x2, matrix products: 19.8 us -> 10.4 us  [the longest x1 8.53 us: per_device(): own_kv = jnp.dot(prompt_rows, piece, preferred_element_type=jnp.float32)]
  transfers between devices with their start and end apart: 4 -> 1, of which waited for: 4 -> 1; matrix products, arithmetic and copies ran while one was open for 2% -> 2% of each run, Pallas kernels for 0% -> 0%
where the time goes in v1:
time: 231 us; the launch traced here: 230 us
  Pallas kernels  100 us (43%)
  matrix products  44.3 us (19%)
  waiting for transfers between devices  39.6 us (17%)
  other arithmetic  23.1 us (10%)
  between operations  14.9 us (6%)
  local copies, waits for them, and re-layouts  7.89 us (3%)
    pallas_call x1, Pallas kernels, finish(): pl.pallas_call(functools.partial(finish_kernel, cols, seqs), out_shape=(j...  76.7 us
    all_gather x1, waiting for transfers between devices, per_device(): prompt_kv = lax.all_gather(own_kv, 'seq', axis=0, tiled=True)  39.6 us
    pallas_call x1, Pallas kernels, gather_weight(): pl.pallas_call(functools.partial(gather_kernel, cols, seqs), out_shape=ja...  23.6 us
    reduce_sum x2, other arithmetic, per_device(): kv_grad = jnp.concatenate([jnp.sum(key_grad, 0), jnp.sum(value_grad, 0)], 1)  9.73 us
    dot_general x4, matrix products, attend_block(): jnp.einsum('htk,thd->kd', probs_b, g_part, preferred_element_type=jnp.flo...  8.55 us
    dot_general x1, matrix products, per_device(): own_kv = jnp.dot(prompt_rows, piece, preferred_element_type=jnp.float32)  8.53 us
    dot_general x4, matrix products, attend_block(): jnp.einsum('htk,thd->kd', dscore, q_part, preferred_element_type=jnp.floa...  8.53 us
    dot_general x4, matrix products, attend_block(): jnp.einsum('htk,kd->thd', probs_b, values, preferred_element_type=jnp.flo...  5.98 us
  transfers between devices with their start and end apart: 1, of which 1 were waited for; matrix products, arithmetic and copies ran while one was open for 2% of the time, Pallas kernels for 0%

profile of v1, /device:TPU:0, one launch (start us, length us, event | category | flops | bytes accessed | tf_op | source)
XLA Modules:
  0.0 230.3 jit_solution(5789792990052175405)
XLA Ops:
  7.2 0.0 all-gather.2.cloned.1.call-start
  7.2 23.6 %gather_weight.1 = bf16[32,160,256]{2,1,0:T(8,128)(2,1)} custom-call(bf16[1,160,256]{2,1,0:T(8,128)(2,1)} %bitcast.145), custom_call_target="tpu_custom_call" | custom-call | tf_op jit(solution)/shard_map/gather_weight/pallas_call | solution.py:83
  30.8 0.0 copy-start.2
  30.8 8.5 %convolution_convert_fusion.1 = bf16[1024,256]{1,0:T(8,128)(2,1)} fusion(bf16[5120,256]{1,0:T(8,128)(2,1)} %bitcast.137, bf16[1,1024,5120]{2,1,0:T(8,128)(2,1)} %param.9), kind=kOutput, calls=%fused_computation.46 | convolution fusion | flops 2684616704 | bytes 13631488 | tf_op jit(solution)/shard_map/dot_general | solution.py:255
  39.4 0.0 all-gather.2.cloned.1.call-update
  40.1 0.2 copy.25
  40.3 1.1 copy.26
  41.4 0.7 fusion.35
  42.1 0.6 iota_compare_fusion.3
  42.8 1.8 convolution_convert_fusion.2
  44.7 0.1 pad_add_fusion
  44.9 39.6 %all-gather.2.cloned.1.call-done = bf16[4096,256]{1,0:T(8,128)(2,1)} async-done(((bf16[1024,256]{1,0:T(8,128)(2,1)}), bf16[4096,256]{1,0:T(8,128)(2,1)}) %all-gather.2.cloned.1.call-update) | async-done | bytes 2097168 | tf_op jit(solution)/shard_map/all_gather | solution.py:259
  84.4 1.7 fusion.39
  86.1 0.0 copy-start.3
  86.1 0.1 pad_maximum_fusion
  86.3 0.8 copy-done.3
  87.1 42.7 %while.17 = (s32[]{:T(128)}, bf16[4,128,2,128]{1,3,2,0:T(8,128)(2,1)}, bf16[4,128,2,128]{3,1,2,0:T(8,128)(2,1)S(1)}, f32[4,4224,128]{2,1,0:T(8,128)}, f32[4,4224...) while((s32[]{:T(128)}, ...), condition=%wide.region_5.6_spmd.clone, body=%wide.region_1.5_spmd.clone.sunk | while | flops 1673072640 | bytes 44391828 | solution.py:304
  87.1 0.6 iota_compare_fusion.5
  87.7 0.9 fusion.79
  88.6 1.1 fusion.80
  89.7 0.3 fusion.81
  90.1 1.5 bitcast_dynamic-update-slice_fusion.2
  91.6 1.1 fusion.82
  92.7 0.7 fusion.83
  93.5 2.1 fusion.84
  95.6 2.2 fusion.85
  97.8 0.6 iota_compare_fusion.5
  98.4 0.9 fusion.79
  99.3 1.1 fusion.80
  100.4 0.3 fusion.81
  100.8 1.5 bitcast_dynamic-update-slice_fusion.2
  102.3 1.1 fusion.82
  103.5 0.7 fusion.83
  104.2 2.1 fusion.84
  106.3 2.1 fusion.85
  108.5 0.6 iota_compare_fusion.5
  109.1 0.8 fusion.79
  110.0 1.1 fusion.80
  111.1 0.3 fusion.81
  111.4 1.5 bitcast_dynamic-update-slice_fusion.2
  113.0 1.1 fusion.82
  114.1 0.7 fusion.83
  114.8 2.1 fusion.84
  117.0 2.1 fusion.85
  119.1 0.6 iota_compare_fusion.5
  119.7 0.9 fusion.79
  120.6 1.1 fusion.80
  121.7 0.3 fusion.81
  122.0 1.5 bitcast_dynamic-update-slice_fusion.2
  123.6 1.1 fusion.82
  124.7 0.7 fusion.83
  125.5 2.1 fusion.84
  127.6 2.1 fusion.85
  129.7 4.2 %reduce_sum.47 = f32[4224,128]{1,0:T(8,128)S(1)} reduce(f32[4,4224,128]{2,1,0:T(8,128)} %get-tuple-element.69, f32[]{:T(128)} %constant.23.clone.1), dimensions={0}, to_apply=%region_7.8 | reduce | flops 1622016 | bytes 10813444 | tf_op jit(solution)/shard_map/reduce_sum | solution.py:307
  133.9 5.6 %reduce_sum.46 = f32[4224,128]{1,0:T(8,128)} reduce(f32[4,4224,128]{2,1,0:T(8,128)} %get-tuple-element.68, f32[]{:T(128)} %constant.23.clone.1), dimensions={0}, to_apply=%region_6.7 | reduce | flops 1622016 | bytes 10813444 | tf_op jit(solution)/shard_map/reduce_sum | solution.py:307
  139.5 1.0 fusion.34.rgrad_ref
  140.5 0.6 copy-done
  141.1 2.2 fusion.33
  143.3 0.8 copy.36
  144.2 76.7 %finish.1 = (bf16[1024,256]{1,0:T(8,128)(2,1)S(1)}, f32[160,256]{1,0:T(8,128)S(1)}) custom-call(f32[4,1024,256]{2,1,0:T(8,128)} %bitcast.136, bf16[128,256]{1,0:T(8,128)(2,1)S(1)} %fusion.34.rgrad_ref, bf16[1024,5120]{1,0:T(8,128)(2,1)} %bitcast.139, bf16[128,5120]{1,0:T(8,128)(2,1)} %bitcast.140), custom_call_target="tpu_custom_call" | custom-call | tf_op jit(solution)/shard_map/finish/pallas_call | solution.py:207
  220.9 0.3 copy.30
  221.1 0.9 broadcast_in_dim_reshape.7
  222.0 0.8 copy.63
  222.8 0.7 copy.64
  (21 shorter events, 0.2 us)
Async XLA Ops:
  7.2 77.3 %all-gather.2.cloned.1.call-start = ((), (), s32[]{:S(2)}) async-start(), calls=%async_computation | async-start | bytes 2621440 | tf_op jit(solution)/shard_map/all_gather | solution.py:259
  30.8 9.3 %copy-start.2 = (bf16[1,128,1024]{2,1,0:T(8,128)(2,1)S(1)}, bf16[1,128,1024]{2,1,0:T(8,128)(2,1)}, u32[]{:S(2)}) copy-start(bf16[1,128,1024]{2,1,0:T(8,128)(2,1)} %param.11) | copy-start | bytes 786436
  30.8 10.6 %copy-start.5 = (s32[1,4]{1,0:T(1,128)S(1)}, s32[1,4]{1,0:T(1,128)}, u32[]{:S(2)}) copy-start(s32[1,4]{1,0:T(1,128)} %param.15) | copy-start | bytes 52
  30.8 12.0 %copy-start.1 = (bf16[32,160,256]{2,1,0:T(8,128)(2,1)S(1)}, bf16[32,160,256]{2,1,0:T(8,128)(2,1)}, u32[]{:S(2)}) copy-start(bf16[32,160,256]{2,1,0:T(8,128)(2,1)} %gather_weight.1) | copy-start | bytes 7864324
  86.1 1.0 copy-start.3
  139.5 1.6 copy-start
  141.1 2.2 copy-start.4
Sparse Core Ops, SparseCore 0:
  39.5 44.8 all-gather.1

commit v2 on v1

--- a/solution.py
+++ b/solution.py
@@ -1,4 +1,5 @@
 import functools
+import math
 
 import jax
 import jax.numpy as jnp
@@ -32,6 +33,41 @@
     return pltpu.make_async_remote_copy(
         src_ref=src, dst_ref=dst, send_sem=send, recv_sem=recv, device_id=device, device_id_type=MESH
     )
+
+
+def encode(x, group):
+    rows, width = x.shape
+    parts = x.reshape(rows // group, group, width)
+    top = jnp.maximum(jnp.max(jnp.abs(parts), 1, keepdims=True), 1e-33)
+    code = jnp.floor(parts * (32000.0 / top) + 0.5).astype(jnp.int32)
+    return code.reshape(rows, width).astype(jnp.int16), (top * (1.0 / 32000.0)).reshape(rows // group, width)
+
+
+def decode(code, scale):
+    rows, width = code.shape
+    groups = scale.shape[0]
+    parts = code.astype(jnp.int32).astype(jnp.float32).reshape(groups, rows // groups, width)
+    return (parts * scale.reshape(groups, 1, width)).reshape(rows, width)
+
+
+class Pair:
+    def __init__(self, codes, scales, sends, recvs, index, device):
+        self.copies = [
+            remote(src.at[index], dst.at[index], sends.at[i, index], recvs.at[i, index], device)
+            for i, (src, dst) in enumerate((codes, scales))
+        ]
+
+    def start(self):
+        for copy in self.copies:
+            copy.start()
+
+    def wait_recv(self):
+        for copy in self.copies:
+            copy.wait_recv()
+
+    def wait_send(self):
+        for copy in self.copies:
+            copy.wait_send()
 
 
 def gather_kernel(cols, seqs, w_ref, out_ref, zs, zr, xs, xr, cs, cr, own_sem):
@@ -102,7 +138,8 @@
 
 def finish_kernel(
     cols, seqs, part_ref, rgrad_ref, x_ref, xr_ref, pgrad_ref, wgrad_ref,
-    xbuf, gt, ksend, krecv, pair, crecv, xsend, xrecv, total, zsend, zrecv,
+    xbuf, gt, ksend, krecv, kscale, kscaled, pair, crecv, xsend, xrecv, xscale, xscaled,
+    total, zsend, zrecv, zscale, zscaled,
     xsem, ks, kr, cs, cr, xs, xr, zs, zr,
 ):
     grp, seq, col, core = place(cols)
@@ -123,9 +160,12 @@
 
     sends = []
     for k in range(1, seqs):
-        ksend[k - 1] = part_ref[(seq + k) % seqs].astype(jnp.bfloat16)
-        copy = remote(
-            ksend.at[k - 1], krecv.at[k - 1], ks.at[k - 1], kr.at[k - 1], (grp, (seq + k) % seqs)
+        for t in range(0, plen, 512):
+            ksend[k - 1, pl.ds(t, 512)], kscale[k - 1, pl.ds(t // 64, 8)] = encode(
+                part_ref[(seq + k) % seqs, pl.ds(t, 512)], 64
+            )
+        copy = Pair(
+            (ksend, krecv), (kscale, kscaled), ks, kr, k - 1, (grp, (seq + k) % seqs)
         )
         copy.start()
         sends.append(copy)
@@ -134,11 +174,11 @@
         load.wait()
     for copy in sends:
         copy.wait_recv()
-    for t in range(0, plen, 256):
-        at = pl.ds(t, 256)
+    for t in range(0, plen, 512):
+        at = pl.ds(t, 512)
         acc = part_ref[seq, at, :]
         for k in range(1, seqs):
-            acc = acc + krecv[k - 1, at, :].astype(jnp.float32)
+            acc = acc + decode(krecv[k - 1, at, :], kscaled[k - 1, pl.ds(t // 64, 8)])
         grad = acc.astype(jnp.bfloat16)
         pgrad_ref[at, :] = grad
         gt[:, at] = grad.astype(jnp.float32).T.astype(jnp.bfloat16)
@@ -151,10 +191,9 @@
 
     def forward(j):
         over[j].wait_recv()
-        xsend[j - 1] = (pair[j, mine, :] + crecv[j]).astype(jnp.bfloat16)
-        copy = remote(
-            xsend.at[j - 1], xrecv.at[j - 1], xs.at[j - 1], xr.at[j - 1],
-            (((col + j) % cols) * CORES + core, seq),
+        xsend[j - 1], xscale[j - 1] = encode(pair[j, mine, :] + crecv[j], 64)
+        copy = Pair(
+            (xsend, xrecv), (xscale, xscaled), xs, xr, j - 1, (((col + j) % cols) * CORES + core, seq)
         )
         copy.start()
         across[j] = copy
@@ -173,21 +212,21 @@
     total[...] = pair[0, mine, :] + crecv[0]
     for j in range(1, cols):
         across[j].wait_recv()
-        total[...] += xrecv[j - 1].astype(jnp.float32)
+        total[...] += decode(xrecv[j - 1], xscaled[j - 1])
 
     last = []
     for k in range(1, seqs):
         at = pl.ds(pl.multiple_of(((seq + k) % seqs) * rows, 8), rows)
-        zsend[k - 1] = total[at, :].astype(jnp.bfloat16)
-        copy = remote(
-            zsend.at[k - 1], zrecv.at[k - 1], zs.at[k - 1], zr.at[k - 1], (grp, (seq + k) % seqs)
+        zsend[k - 1], zscale[k - 1] = encode(total[at, :], math.gcd(rows, 32))
+        copy = Pair(
+            (zsend, zrecv), (zscale, zscaled), zs, zr, k - 1, (grp, (seq + k) % seqs)
         )
         copy.start()
         last.append(copy)
     acc = total[pl.ds(pl.multiple_of(seq * rows, 8), rows), :]
     for k in range(1, seqs):
         last[k - 1].wait_recv()
-        acc = acc + zrecv[k - 1].astype(jnp.float32)
+        acc = acc + decode(zrecv[k - 1], zscaled[k - 1])
     wgrad_ref[...] = acc
     for copy in sends + list(over.values()) + list(across.values()) + last:
         copy.wait_send()
@@ -200,7 +239,7 @@
     block = d // cols
     half = block // CORES
     rows = half // seqs
-    bf16, f32 = jnp.bfloat16, jnp.float32
+    bf16, f32, i16 = jnp.bfloat16, jnp.float32, jnp.int16
     vmem = pl.BlockSpec(memory_space=pltpu.VMEM)
     hbm = pl.BlockSpec(memory_space=pl.ANY)
     dma = pltpu.SemaphoreType.DMA
@@ -215,20 +254,26 @@
         scratch_shapes=[
             pltpu.VMEM((cols, plen + rt, block), bf16),
             pltpu.VMEM((width, plen + rt), bf16),
-            pltpu.VMEM((seqs - 1, plen, width), bf16),
-            pltpu.VMEM((seqs - 1, plen, width), bf16),
+            pltpu.VMEM((seqs - 1, plen, width), i16),
+            pltpu.VMEM((seqs - 1, plen, width), i16),
+            pltpu.VMEM((seqs - 1, plen // 64, width), f32),
+            pltpu.VMEM((seqs - 1, plen // 64, width), f32),
             pltpu.VMEM((cols, block, width), f32),
             pltpu.VMEM((cols, half, width), f32),
-            pltpu.VMEM((cols - 1, half, width), bf16),
-            pltpu.VMEM((cols - 1, half, width), bf16),
+            pltpu.VMEM((cols - 1, half, width), i16),
+            pltpu.VMEM((cols - 1, half, width), i16),
+            pltpu.VMEM((cols - 1, half // 64, width), f32),
+            pltpu.VMEM((cols - 1, half // 64, width), f32),
             pltpu.VMEM((half, width), f32),
-            pltpu.VMEM((seqs - 1, rows, width), bf16),
-            pltpu.VMEM((seqs - 1, rows, width), bf16),
+            pltpu.VMEM((seqs - 1, rows, width), i16),
+            pltpu.VMEM((seqs - 1, rows, width), i16),
+            pltpu.VMEM((seqs - 1, rows // math.gcd(rows, 32), width), f32),
+            pltpu.VMEM((seqs - 1, rows // math.gcd(rows, 32), width), f32),
             dma((2, cols)),
-            dma((seqs - 1,)), dma((seqs - 1,)),
+            dma((2, seqs - 1)), dma((2, seqs - 1)),
             dma((cols,)), dma((cols,)),
-            dma((cols - 1,)), dma((cols - 1,)),
-            dma((seqs - 1,)), dma((seqs - 1,)),
+            dma((2, cols - 1)), dma((2, cols - 1)),
+            dma((2, seqs - 1)), dma((2, seqs - 1)),
         ],
         compiler_params=pltpu.CompilerParams(
             collective_id=1, has_side_effects=True, vmem_limit_bytes=52 * 2**20

time: 231 us -> 234 us (1.013)
  Pallas kernels: 100 us -> 104 us
    pallas_call x1, Pallas kernels: 76.7 us -> 80.4 us  [finish(): pl.pallas_call(functools.partial(finish_kernel, cols, seqs), out_shape=(j...]
where the time goes in v2:
time: 234 us
  Pallas kernels  104 us (44%)
  matrix products  44.3 us (19%)
  waiting for transfers between devices  39.6 us (17%)
  other arithmetic  23.1 us (10%)
  between operations  14.9 us (6%)
  local copies, waits for them, and re-layouts  7.89 us (3%)
    pallas_call x1, Pallas kernels, finish(): pl.pallas_call(functools.partial(finish_kernel, cols, seqs), out_shape=(j...  80.4 us
    all_gather x1, waiting for transfers between devices, per_device(): prompt_kv = lax.all_gather(own_kv, 'seq', axis=0, tiled=True)  39.6 us
    pallas_call x1, Pallas kernels, gather_weight(): pl.pallas_call(functools.partial(gather_kernel, cols, seqs), out_shape=ja...  23.6 us
    reduce_sum x2, other arithmetic, per_device(): kv_grad = jnp.concatenate([jnp.sum(key_grad, 0), jnp.sum(value_grad, 0)], 1)  9.73 us
    dot_general x4, matrix products, attend_block(): jnp.einsum('htk,thd->kd', probs_b, g_part, preferred_element_type=jnp.flo...  8.55 us
    dot_general x1, matrix products, per_device(): own_kv = jnp.dot(prompt_rows, piece, preferred_element_type=jnp.float32)  8.53 us
    dot_general x4, matrix products, attend_block(): jnp.einsum('htk,thd->kd', dscore, q_part, preferred_element_type=jnp.floa...  8.53 us
    dot_general x4, matrix products, attend_block(): jnp.einsum('htk,kd->thd', probs_b, values, preferred_element_type=jnp.flo...  5.98 us
  transfers between devices with their start and end apart: 1, of which 1 were waited for; matrix products, arithmetic and copies ran while one was open for 2% of the time, Pallas kernels for 0%

profile of v2, /device:TPU:0, one launch (start us, length us, event | category | flops | bytes accessed | tf_op | source)
XLA Modules:
  0.0 234.0 jit_solution(17426823988505699583)
XLA Ops:
  7.2 0.0 all-gather.2.cloned.1.call-start
  7.2 23.6 %gather_weight.1 = bf16[32,160,256]{2,1,0:T(8,128)(2,1)} custom-call(bf16[1,160,256]{2,1,0:T(8,128)(2,1)} %bitcast.145), custom_call_target="tpu_custom_call" | custom-call | tf_op jit(solution)/shard_map/gather_weight/pallas_call | solution.py:119
  30.8 0.0 copy-start.2
  30.8 8.5 %convolution_convert_fusion.1 = bf16[1024,256]{1,0:T(8,128)(2,1)} fusion(bf16[5120,256]{1,0:T(8,128)(2,1)} %bitcast.137, bf16[1,1024,5120]{2,1,0:T(8,128)(2,1)} %param.9), kind=kOutput, calls=%fused_computation.46 | convolution fusion | flops 2684616704 | bytes 13631488 | tf_op jit(solution)/shard_map/dot_general | solution.py:300
  39.4 0.0 all-gather.2.cloned.1.call-update
  40.1 0.2 copy.25
  40.3 1.1 copy.26
  41.4 0.7 fusion.35
  42.1 0.6 iota_compare_fusion.3
  42.8 1.8 convolution_convert_fusion.2
  44.7 0.1 pad_add_fusion
  44.9 39.6 %all-gather.2.cloned.1.call-done = bf16[4096,256]{1,0:T(8,128)(2,1)} async-done(((bf16[1024,256]{1,0:T(8,128)(2,1)}), bf16[4096,256]{1,0:T(8,128)(2,1)}) %all-gather.2.cloned.1.call-update) | async-done | bytes 2097168 | tf_op jit(solution)/shard_map/all_gather | solution.py:304
  84.4 1.7 fusion.39
  86.1 0.0 copy-start.3
  86.1 0.1 pad_maximum_fusion
  86.3 0.8 copy-done.3
  87.1 42.7 %while.17 = (s32[]{:T(128)}, bf16[4,128,2,128]{1,3,2,0:T(8,128)(2,1)}, bf16[4,128,2,128]{3,1,2,0:T(8,128)(2,1)S(1)}, f32[4,4224,128]{2,1,0:T(8,128)}, f32[4,4224...) while((s32[]{:T(128)}, ...), condition=%wide.region_5.6_spmd.clone, body=%wide.region_1.5_spmd.clone.sunk | while | flops 1673072640 | bytes 44391828 | solution.py:349
  87.1 0.6 iota_compare_fusion.5
  87.7 0.9 fusion.79
  88.6 1.1 fusion.80
  89.7 0.3 fusion.81
  90.1 1.5 bitcast_dynamic-update-slice_fusion.2
  91.6 1.1 fusion.82
  92.7 0.7 fusion.83
  93.5 2.1 fusion.84
  95.6 2.2 fusion.85
  97.8 0.6 iota_compare_fusion.5
  98.4 0.9 fusion.79
  99.3 1.1 fusion.80
  100.4 0.3 fusion.81
  100.8 1.5 bitcast_dynamic-update-slice_fusion.2
  102.3 1.1 fusion.82
  103.5 0.7 fusion.83
  104.2 2.1 fusion.84
  106.3 2.1 fusion.85
  108.5 0.6 iota_compare_fusion.5
  109.1 0.8 fusion.79
  110.0 1.1 fusion.80
  111.1 0.3 fusion.81
  111.4 1.5 bitcast_dynamic-update-slice_fusion.2
  113.0 1.1 fusion.82
  114.1 0.7 fusion.83
  114.8 2.1 fusion.84
  117.0 2.1 fusion.85
  119.1 0.6 iota_compare_fusion.5
  119.7 0.9 fusion.79
  120.6 1.1 fusion.80
  121.7 0.3 fusion.81
  122.0 1.5 bitcast_dynamic-update-slice_fusion.2
  123.6 1.1 fusion.82
  124.7 0.7 fusion.83
  125.5 2.1 fusion.84
  127.6 2.1 fusion.85
  129.7 4.2 %reduce_sum.47 = f32[4224,128]{1,0:T(8,128)S(1)} reduce(f32[4,4224,128]{2,1,0:T(8,128)} %get-tuple-element.69, f32[]{:T(128)} %constant.23.clone.1), dimensions={0}, to_apply=%region_7.8 | reduce | flops 1622016 | bytes 10813444 | tf_op jit(solution)/shard_map/reduce_sum | solution.py:352
  133.9 5.6 %reduce_sum.46 = f32[4224,128]{1,0:T(8,128)} reduce(f32[4,4224,128]{2,1,0:T(8,128)} %get-tuple-element.68, f32[]{:T(128)} %constant.23.clone.1), dimensions={0}, to_apply=%region_6.7 | reduce | flops 1622016 | bytes 10813444 | tf_op jit(solution)/shard_map/reduce_sum | solution.py:352
  139.5 1.0 fusion.34.rgrad_ref
  140.5 0.6 copy-done
  141.1 2.2 fusion.33
  143.3 0.8 copy.36
  144.2 80.4 %finish.1 = (bf16[1024,256]{1,0:T(8,128)(2,1)S(1)}, f32[160,256]{1,0:T(8,128)S(1)}) custom-call(f32[4,1024,256]{2,1,0:T(8,128)} %bitcast.136, bf16[128,256]{1,0:T(8,128)(2,1)S(1)} %fusion.34.rgrad_ref, bf16[1024,5120]{1,0:T(8,128)(2,1)} %bitcast.139, bf16[128,5120]{1,0:T(8,128)(2,1)} %bitcast.140), custom_call_target="tpu_custom_call" | custom-call | tf_op jit(solution)/shard_map/finish/pallas_call | solution.py:246
  224.6 0.3 copy.30
  224.8 0.9 broadcast_in_dim_reshape.7
  225.7 0.8 copy.63
  226.5 0.7 copy.64
  (21 shorter events, 0.2 us)
Async XLA Ops:
  7.2 77.3 %all-gather.2.cloned.1.call-start = ((), (), s32[]{:S(2)}) async-start(), calls=%async_computation | async-start | bytes 2621440 | tf_op jit(solution)/shard_map/all_gather | solution.py:304
  30.8 9.3 %copy-start.2 = (bf16[1,128,1024]{2,1,0:T(8,128)(2,1)S(1)}, bf16[1,128,1024]{2,1,0:T(8,128)(2,1)}, u32[]{:S(2)}) copy-start(bf16[1,128,1024]{2,1,0:T(8,128)(2,1)} %param.11) | copy-start | bytes 786436
  30.8 10.6 %copy-start.5 = (s32[1,4]{1,0:T(1,128)S(1)}, s32[1,4]{1,0:T(1,128)}, u32[]{:S(2)}) copy-start(s32[1,4]{1,0:T(1,128)} %param.15) | copy-start | bytes 52
  30.8 12.0 %copy-start.1 = (bf16[32,160,256]{2,1,0:T(8,128)(2,1)S(1)}, bf16[32,160,256]{2,1,0:T(8,128)(2,1)}, u32[]{:S(2)}) copy-start(bf16[32,160,256]{2,1,0:T(8,128)(2,1)} %gather_weight.1) | copy-start | bytes 7864324
  86.1 1.0 copy-start.3
  139.5 1.6 copy-start
  141.1 2.2 copy-start.4
Sparse Core Ops, SparseCore 0:
  39.5 44.8 all-gather.1

commit v3 on v2

--- a/solution.py
+++ b/solution.py
@@ -282,76 +282,141 @@
     )(part, rgrad, x, xr)
 
 
+def attend_kernel(
+    lens_ref, q_ref, g_ref, kv_ref, rkv_ref, out_ref, qg_ref, part_ref, rgrad_ref, kvt, score, rpart
+):
+    step = pl.program_id(0)
+    f32, bf16 = jnp.float32, jnp.bfloat16
+    slots = q_ref.shape[0]
+    dim = rkv_ref.shape[1] // 2
+    chunk = 512
+    chunks = kv_ref.shape[0] // chunk
+    scale = dim ** (-0.5)
+    prompt_len, resp_len = lens_ref[0], lens_ref[1]
+
+    def rows(c):
+        return pl.ds(pl.multiple_of(c * chunk, chunk), chunk)
+
+    @pl.when(step == 0)
+    def _():
+        def init(c, carry):
+            kvt[:, rows(c)] = kv_ref[rows(c), :].T
+            part_ref[rows(c), :] = jnp.zeros((chunk, 2 * dim), f32)
+            return carry
+
+        lax.fori_loop(0, chunks, init, 0)
+        rpart[...] = jnp.zeros_like(rpart)
+
+    q2 = jnp.concatenate([q_ref[:, :dim], q_ref[:, dim:]], 0)
+    g2 = jnp.concatenate([g_ref[:, :dim], g_ref[:, dim:]], 0)
+    live = lax.broadcasted_iota(jnp.int32, g2.shape, 0) % slots < resp_len
+    g32 = jnp.where(live, g2.astype(f32), 0.0)
+    g2 = g32.astype(bf16)
+    rows_by = (((1,), (1,)), ((), ()))
+
+    def dot_nt(a, b):
+        return lax.dot_general(a, b, rows_by, preferred_element_type=f32)
+
+    def dot(a, b):
+        return jnp.dot(a, b, preferred_element_type=f32)
+
+    rkeys, rvalues = rkv_ref[:, :dim], rkv_ref[:, dim:]
+    rscore = dot_nt(rkeys, q2) * scale
+    at_key = lax.broadcasted_iota(jnp.int32, rscore.shape, 0)
+    at_slot = lax.broadcasted_iota(jnp.int32, rscore.shape, 1) % slots
+    rscore = jnp.where(at_key <= at_slot, rscore, -jnp.inf)
+
+    def scores(c, top):
+        s = dot_nt(kv_ref[rows(c), :dim], q2) * scale
+        at = lax.broadcasted_iota(jnp.int32, s.shape, 0) + c * chunk
+        s = jnp.where(at < prompt_len, s, -jnp.inf)
+        score[rows(c), :] = s
+        return jnp.maximum(top, jnp.max(s, 0, keepdims=True))
+
+    top = lax.fori_loop(0, chunks, scores, jnp.max(rscore, 0, keepdims=True))
+    rexpo = jnp.exp(rscore - top)
+
+    def expos(c, total):
+        e = jnp.exp(score[rows(c), :] - top)
+        score[rows(c), :] = e
+        return total + jnp.sum(e, 0, keepdims=True)
+
+    total = lax.fori_loop(0, chunks, expos, jnp.sum(rexpo, 0, keepdims=True))
+    inverse = 1.0 / total
+    rprobs_b = (rexpo * inverse).astype(bf16)
+    rpart[:, dim:] += dot(rprobs_b, g2)
+
+    def attend(c, acc):
+        probs_b = (score[rows(c), :] * inverse).astype(bf16)
+        part_ref[rows(c), dim:] += dot(probs_b, g2)
+        return acc + dot(kvt[dim:, rows(c)], probs_b)
+
+    acc = lax.fori_loop(0, chunks, attend, dot(rvalues.astype(f32).T.astype(bf16), rprobs_b))
+    out = jnp.where(live, acc.T, 0.0).astype(bf16)
+    out_ref[...] = jnp.concatenate([out[:slots], out[slots:]], 1)
+    delta = jnp.sum(g32.T * out.astype(f32).T, 0, keepdims=True)
+    scaled = inverse * scale
+    rdscore = (rexpo * scaled * (dot_nt(rvalues, g2) - delta)).astype(bf16)
+    rpart[:, :dim] += dot(rdscore, q2)
+
+    def back(c, acc):
+        dprob = dot_nt(kv_ref[rows(c), dim:], g2)
+        dscore = (score[rows(c), :] * scaled * (dprob - delta)).astype(bf16)
+        part_ref[rows(c), :dim] += dot(dscore, q2)
+        return acc + dot(kvt[:dim, rows(c)], dscore)
+
+    acc = lax.fori_loop(0, chunks, back, dot(rkeys.astype(f32).T.astype(bf16), rdscore))
+    grad = acc.T.astype(bf16)
+    qg_ref[...] = jnp.concatenate([grad[:slots], grad[slots:]], 1)
+    rgrad_ref[...] = rpart[...].astype(bf16)
+
+
+def attend(lens, q, g, kv, rkv):
+    slots, width = q.shape
+    plen, kv_width = kv.shape
+    bf16, f32 = jnp.bfloat16, jnp.float32
+    heads = pl.BlockSpec((slots, kv_width), lambda i: (0, i))
+
+    def whole(rows):
+        return pl.BlockSpec((rows, kv_width), lambda i: (0, 0))
+
+    return pl.pallas_call(
+        attend_kernel,
+        grid=(width // kv_width,),
+        out_shape=(
+            jax.ShapeDtypeStruct((slots, width), bf16),
+            jax.ShapeDtypeStruct((slots, width), bf16),
+            jax.ShapeDtypeStruct((plen, kv_width), f32),
+            jax.ShapeDtypeStruct((slots, kv_width), bf16),
+        ),
+        in_specs=[pl.BlockSpec(memory_space=pltpu.SMEM), heads, heads, whole(plen), whole(slots)],
+        out_specs=(heads, heads, whole(plen), whole(slots)),
+        scratch_shapes=[
+            pltpu.VMEM((kv_width, plen), bf16),
+            pltpu.VMEM((plen, 2 * slots), f32),
+            pltpu.VMEM((slots, kv_width), f32),
+        ],
+        compiler_params=pltpu.CompilerParams(vmem_limit_bytes=52 * 2**20),
+        name="attend",
+    )(lens, q, g, kv, rkv)
+
+
 def per_device(
     cols, seqs,
     prompt_hidden, resp_hidden, queries, grad_out, kv_weight, prompt_lengths, response_lengths
 ):
     seq_rank = lax.axis_index("seq")
-    head_dim = kv_weight.shape[1] // 2
-    rt_dev = resp_hidden.shape[1]
-    width = queries.shape[2]
-    heads = width // head_dim
-    group_heads = 2
-    blocks = heads // group_heads
-    scale = head_dim ** (-0.5)
     prompt_rows = prompt_hidden[0]
     resp_rows = resp_hidden[0]
     piece = gather_weight(kv_weight, cols, seqs)
-    own_kv = jnp.dot(prompt_rows, piece, preferred_element_type=jnp.float32)
-    resp_kv = jnp.dot(resp_rows, piece, preferred_element_type=jnp.float32)
-    own_kv = own_kv.astype(jnp.bfloat16)
-    resp_kv = resp_kv.astype(jnp.bfloat16)
+    own_kv = jnp.dot(prompt_rows, piece, preferred_element_type=jnp.float32).astype(jnp.bfloat16)
+    resp_kv = jnp.dot(resp_rows, piece, preferred_element_type=jnp.float32).astype(jnp.bfloat16)
     prompt_kv = lax.all_gather(own_kv, "seq", axis=0, tiled=True)
-    plen_all = prompt_kv.shape[0]
-    prompt_len = prompt_lengths[0]
-    lengths_row = response_lengths[0]
-    members = jnp.arange(lengths_row.shape[0])
-    resp_len = jnp.sum(jnp.where(members == seq_rank, lengths_row, 0))
-    position = jnp.arange(rt_dev)
-    live = position < resp_len
-    prompt_ok = jnp.arange(plen_all) < prompt_len
-    allowed = jnp.concatenate(
-        [
-            jnp.broadcast_to(prompt_ok[None, :], (rt_dev, plen_all)),
-            position[None, :] <= position[:, None],
-        ],
-        1,
-    )
-    keys = jnp.concatenate([prompt_kv[:, :head_dim], resp_kv[:, :head_dim]], 0)
-    values = jnp.concatenate([prompt_kv[:, head_dim:], resp_kv[:, head_dim:]], 0)
-    grad_live = jnp.where(live[:, None], grad_out[0], jnp.zeros_like(grad_out[0]))
-    q_blocks = queries[0].reshape(rt_dev, blocks, group_heads, head_dim).transpose(1, 0, 2, 3)
-    g_blocks = grad_live.reshape(rt_dev, blocks, group_heads, head_dim).transpose(1, 0, 2, 3)
-
-    def attend_block(pieces):
-        q_part, g_part = pieces
-        scores = jnp.einsum("thd,kd->htk", q_part, keys, preferred_element_type=jnp.float32) * scale
-        scores = jnp.where(allowed[None], scores, -jnp.inf)
-        top = jnp.max(scores, 2, keepdims=True)
-        expo = jnp.exp(scores - top)
-        total = jnp.sum(expo, 2, keepdims=True)
-        probs = expo / total
-        probs_b = probs.astype(jnp.bfloat16)
-        out_part = jnp.einsum("htk,kd->thd", probs_b, values, preferred_element_type=jnp.float32)
-        out_part = jnp.where(live[:, None, None], out_part, jnp.zeros_like(out_part)).astype(
-            jnp.bfloat16
-        )
-        delta = jnp.sum(g_part.astype(jnp.float32) * out_part.astype(jnp.float32), 2).T
-        dprob = jnp.einsum("thd,kd->htk", g_part, values, preferred_element_type=jnp.float32)
-        dscore = (probs * (dprob - delta[:, :, None]) * scale).astype(jnp.bfloat16)
-        q_grad = jnp.einsum("htk,kd->thd", dscore, keys, preferred_element_type=jnp.float32).astype(
-            jnp.bfloat16
-        )
-        key_grad = jnp.einsum("htk,thd->kd", dscore, q_part, preferred_element_type=jnp.float32)
-        value_grad = jnp.einsum("htk,thd->kd", probs_b, g_part, preferred_element_type=jnp.float32)
-        return (out_part, q_grad, key_grad, value_grad)
-
-    out_b, qg_b, key_grad, value_grad = lax.map(attend_block, (q_blocks, g_blocks))
-    attended = out_b.transpose(1, 0, 2, 3).reshape(rt_dev, width)
-    query_grad = qg_b.transpose(1, 0, 2, 3).reshape(rt_dev, width)
-    kv_grad = jnp.concatenate([jnp.sum(key_grad, 0), jnp.sum(value_grad, 0)], 1)
-    resp_grad = kv_grad[plen_all:].astype(jnp.bfloat16)
-    part = kv_grad[:plen_all].reshape(seqs, plen_all // seqs, 2 * head_dim)
+    members = jnp.arange(response_lengths.shape[1])
+    resp_len = jnp.sum(jnp.where(members == seq_rank, response_lengths[0], 0))
+    lens = jnp.stack([prompt_lengths[0], resp_len])
+    attended, query_grad, part, resp_grad = attend(lens, queries[0], grad_out[0], prompt_kv, resp_kv)
+    part = part.reshape(seqs, part.shape[0] // seqs, part.shape[1])
     prompt_grad, weight_grad = finish(part, resp_grad, prompt_rows, resp_rows, cols, seqs)
     return (attended[None], query_grad[None], prompt_grad[None], weight_grad)
 

time: 234 us -> 216 us (0.923)
  Pallas kernels: 104 us -> 146 us
  matrix products: 44.3 us -> 10.4 us
  other arithmetic: 23.1 us -> 1.35 us
  local copies, waits for them, and re-layouts: 7.89 us -> 1.48 us
    pallas_call x0 -> x1, Pallas kernels: none -> 42.1 us  [attend(): pl.pallas_call(attend_kernel, grid=(width // kv_width,), out_shape=(jax.S...]
    dot_general x26 -> x2, matrix products: 44.3 us -> 10.4 us  [the longest x1 8.54 us: per_device(): jnp.dot(prompt_rows, piece, preferred_element_type=jnp.float32)]
    reduce_sum x7 -> x1, other arithmetic: 10.6 us -> 0.63 us  [per_device(): resp_len = jnp.sum(jnp.where(members == seq_rank, response_lengths[0], 0))]
    sub x4 -> x0, other arithmetic: 4.48 us -> none  [attend_block(): expo = jnp.exp(scores - top)]
    lt x6 -> x0, other arithmetic: 3.2 us -> none  [the longest x5 3.19 us: per_device(): live = position < resp_len]
    unnamed x16 -> x10, local copies, waits for them, and re-layouts: 4.21 us -> 1.48 us
    concatenate x3 -> x0, other arithmetic: 2.48 us -> none  [the longest x1 2.19 us: per_device(): kv_grad = jnp.concatenate([jnp.sum(key_grad, 0), jnp.sum(value_grad, 0)], 1)]
  transfers between devices with their start and end apart: 1 -> 1, of which waited for: 1 -> 1; matrix products, arithmetic and copies ran while one was open for 2% -> 1% of each run, Pallas kernels for 0% -> 0%
where the time goes in v3:
time: 216 us; the launch traced here: 215 us
  Pallas kernels  146 us (68%)
  waiting for transfers between devices  41.2 us (19%)
  between operations  14.8 us (7%)
  matrix products  10.4 us (5%)
    pallas_call x1, Pallas kernels, finish(): pl.pallas_call(functools.partial(finish_kernel, cols, seqs), out_shape=(j...  80.5 us
    pallas_call x1, Pallas kernels, attend(): pl.pallas_call(attend_kernel, grid=(width // kv_width,), out_shape=(jax.S...  42.1 us
    all_gather x1, waiting for transfers between devices, per_device(): prompt_kv = lax.all_gather(own_kv, 'seq', axis=0, tiled=True)  41.1 us
    pallas_call x1, Pallas kernels, gather_weight(): pl.pallas_call(functools.partial(gather_kernel, cols, seqs), out_shape=ja...  23.6 us
    dot_general x1, matrix products, per_device(): jnp.dot(prompt_rows, piece, preferred_element_type=jnp.float32)  8.54 us
  transfers between devices with their start and end apart: 1, of which 1 were waited for; matrix products, arithmetic and copies ran while one was open for 1% of the time, Pallas kernels for 0%

profile of v3, /device:TPU:0, one launch (start us, length us, event | category | flops | bytes accessed | tf_op | source)
XLA Modules:
  0.0 215.4 jit_solution(4032882633158011309)
XLA Ops:
  7.2 0.0 all-gather.2.cloned.1.call-start
  7.2 23.6 %gather_weight.1 = bf16[32,160,256]{2,1,0:T(8,128)(2,1)} custom-call(bf16[1,160,256]{2,1,0:T(8,128)(2,1)} %bitcast.27), custom_call_target="tpu_custom_call" | custom-call | tf_op jit(solution)/shard_map/gather_weight/pallas_call | solution.py:119
  30.8 0.0 copy-start.3
  30.8 0.0 copy-start.2
  30.8 8.5 %convolution_convert_fusion = bf16[1024,256]{1,0:T(8,128)(2,1)} fusion(bf16[5120,256]{1,0:T(8,128)(2,1)} %bitcast.22, bf16[1,1024,5120]{2,1,0:T(8,128)(2,1)} %param.7), kind=kOutput, calls=%fused_computation | convolution fusion | flops 2684616704 | bytes 13631488 | tf_op jit(solution)/shard_map/dot_general | solution.py:412
  39.4 0.0 copy-start
  39.4 0.0 copy-start.1
  39.4 0.0 all-gather.2.cloned.1.call-update
  40.1 0.0 copy-done.3
  40.1 0.6 fusion
  40.7 0.7 pad_add_fusion.lens_ref
  41.5 0.0 copy-done.2
  41.5 1.8 convolution_convert_fusion.1.rkv_ref
  43.3 41.1 %all-gather.2.cloned.1.call-done.kv_ref = bf16[4096,256]{1,0:T(8,128)(2,1)} async-done(((bf16[1024,256]{1,0:T(8,128)(2,1)}), bf16[4096,256]{1,0:T(8,128)(2,1)}) %all-gather.2.cloned.1.call-update) | async-done | bytes 2097168 | tf_op jit(solution)/shard_map/all_gather | solution.py:414
  84.4 0.0 copy-done
  84.4 0.0 copy-done.1
  84.4 42.1 %attend.1 = (bf16[128,1024]{1,0:T(8,128)(2,1)}, bf16[128,1024]{1,0:T(8,128)(2,1)}, f32[4096,256]{1,0:T(8,128)}, bf16[128,256]{1,0:T(8,128)(2,1)S(1)}) custom-call(s32[2]{0:T(128)S(1)} %pad_add_fusion.lens_ref, bf16[128,1024]{1,0:T(8,128)(2,1)S(1)} %bitcast.20, bf16[128,1024]{1,0:T(8,128)(2,1)S(1)} %bitcast.21, ...), custom_call_target="tpu_custom_call" | custom-call | tf_op jit(solution)/shard_map/attend/pallas_call | solution.py:383
  126.6 80.5 %finish.1 = (bf16[1024,256]{1,0:T(8,128)(2,1)S(1)}, f32[160,256]{1,0:T(8,128)S(1)}) custom-call(f32[4,1024,256]{2,1,0:T(8,128)} %bitcast.26, bf16[128,256]{1,0:T(8,128)(2,1)S(1)} %get-tuple-element.13.rgrad_ref, bf16[1024,5120]{1,0:T(8,128)(2,1)} %bitcast.24, bf16[128,5120]{1,0:T(8,128)(2,1)} %bitcast.25), custom_call_target="tpu_custom_call" | custom-call | tf_op jit(solution)/shard_map/finish/pallas_call | solution.py:246
  207.1 0.8 copy.14
  207.9 0.7 copy.15
Async XLA Ops:
  7.2 77.3 %all-gather.2.cloned.1.call-start = ((), (), s32[]{:S(2)}) async-start(), calls=%async_computation | async-start | bytes 2621440 | tf_op jit(solution)/shard_map/all_gather | solution.py:414
  30.8 9.3 %copy-start.3 = (s32[1,4]{1,0:T(1,128)S(1)}, s32[1,4]{1,0:T(1,128)}, u32[]{:S(2)}) copy-start(s32[1,4]{1,0:T(1,128)} %param.13) | copy-start | bytes 52
  30.8 10.6 %copy-start.2 = (bf16[32,160,256]{2,1,0:T(8,128)(2,1)S(1)}, bf16[32,160,256]{2,1,0:T(8,128)(2,1)}, u32[]{:S(2)}) copy-start(bf16[32,160,256]{2,1,0:T(8,128)(2,1)} %gather_weight.1) | copy-start | bytes 7864324
  39.4 45.1 %copy-start = (bf16[1,128,1024]{2,1,0:T(8,128)(2,1)S(1)}, bf16[1,128,1024]{2,1,0:T(8,128)(2,1)}, u32[]{:S(2)}) copy-start(bf16[1,128,1024]{2,1,0:T(8,128)(2,1)} %param.9) | copy-start | bytes 786436
  39.4 45.1 %copy-start.1 = (bf16[1,128,1024]{2,1,0:T(8,128)(2,1)S(1)}, bf16[1,128,1024]{2,1,0:T(8,128)(2,1)}, u32[]{:S(2)}) copy-start(bf16[1,128,1024]{2,1,0:T(8,128)(2,1)} %param.10) | copy-start | bytes 786436
Sparse Core Ops, SparseCore 0:
  39.5 44.8 all-gather.1

commit v4 on v3

--- a/solution.py
+++ b/solution.py
@@ -333,7 +333,7 @@
         score[rows(c), :] = s
         return jnp.maximum(top, jnp.max(s, 0, keepdims=True))
 
-    top = lax.fori_loop(0, chunks, scores, jnp.max(rscore, 0, keepdims=True))
+    top = lax.fori_loop(0, chunks, scores, jnp.max(rscore, 0, keepdims=True), unroll=4)
     rexpo = jnp.exp(rscore - top)
 
     def expos(c, total):
@@ -341,7 +341,7 @@
         score[rows(c), :] = e
         return total + jnp.sum(e, 0, keepdims=True)
 
-    total = lax.fori_loop(0, chunks, expos, jnp.sum(rexpo, 0, keepdims=True))
+    total = lax.fori_loop(0, chunks, expos, jnp.sum(rexpo, 0, keepdims=True), unroll=4)
     inverse = 1.0 / total
     rprobs_b = (rexpo * inverse).astype(bf16)
     rpart[:, dim:] += dot(rprobs_b, g2)
@@ -351,7 +351,7 @@
         part_ref[rows(c), dim:] += dot(probs_b, g2)
         return acc + dot(kvt[dim:, rows(c)], probs_b)
 
-    acc = lax.fori_loop(0, chunks, attend, dot(rvalues.astype(f32).T.astype(bf16), rprobs_b))
+    acc = lax.fori_loop(0, chunks, attend, dot(rvalues.astype(f32).T.astype(bf16), rprobs_b), unroll=4)
     out = jnp.where(live, acc.T, 0.0).astype(bf16)
     out_ref[...] = jnp.concatenate([out[:slots], out[slots:]], 1)
     delta = jnp.sum(g32.T * out.astype(f32).T, 0, keepdims=True)
@@ -365,7 +365,7 @@
         part_ref[rows(c), :dim] += dot(dscore, q2)
         return acc + dot(kvt[:dim, rows(c)], dscore)
 
-    acc = lax.fori_loop(0, chunks, back, dot(rkeys.astype(f32).T.astype(bf16), rdscore))
+    acc = lax.fori_loop(0, chunks, back, dot(rkeys.astype(f32).T.astype(bf16), rdscore), unroll=4)
     grad = acc.T.astype(bf16)
     qg_ref[...] = jnp.concatenate([grad[:slots], grad[slots:]], 1)
     rgrad_ref[...] = rpart[...].astype(bf16)

time: 216 us -> 202 us (0.935)
  Pallas kernels: 146 us -> 133 us
    pallas_call x1, Pallas kernels: 42.1 us -> 28.9 us  [attend(): pl.pallas_call(attend_kernel, grid=(width // kv_width,), out_shape=(jax.S...]
  transfers between devices with their start and end apart: 1 -> 1, of which waited for: 1 -> 1; matrix products, arithmetic and copies ran while one was open for 1% -> 2% of each run, Pallas kernels for 0% -> 0%
where the time goes in v4:
time: 202 us
  Pallas kernels  133 us (66%)
  waiting for transfers between devices  41.2 us (20%)
  between operations  14.8 us (7%)
  matrix products  10.4 us (5%)
    pallas_call x1, Pallas kernels, finish(): pl.pallas_call(functools.partial(finish_kernel, cols, seqs), out_shape=(j...  80.5 us
    all_gather x1, waiting for transfers between devices, per_device(): prompt_kv = lax.all_gather(own_kv, 'seq', axis=0, tiled=True)  41.1 us
    pallas_call x1, Pallas kernels, attend(): pl.pallas_call(attend_kernel, grid=(width // kv_width,), out_shape=(jax.S...  28.9 us
    pallas_call x1, Pallas kernels, gather_weight(): pl.pallas_call(functools.partial(gather_kernel, cols, seqs), out_shape=ja...  23.6 us
    dot_general x1, matrix products, per_device(): jnp.dot(prompt_rows, piece, preferred_element_type=jnp.float32)  8.53 us
  transfers between devices with their start and end apart: 1, of which 1 were waited for; matrix products, arithmetic and copies ran while one was open for 2% of the time, Pallas kernels for 0%

profile of v4, /device:TPU:0, one launch (start us, length us, event | category | flops | bytes accessed | tf_op | source)
XLA Modules:
  0.0 202.2 jit_solution(11597767425471266605)
XLA Ops:
  7.2 0.0 all-gather.2.cloned.1.call-start
  7.2 23.6 %gather_weight.1 = bf16[32,160,256]{2,1,0:T(8,128)(2,1)} custom-call(bf16[1,160,256]{2,1,0:T(8,128)(2,1)} %bitcast.27), custom_call_target="tpu_custom_call" | custom-call | tf_op jit(solution)/shard_map/gather_weight/pallas_call | solution.py:119
  30.8 0.0 copy-start.3
  30.8 0.0 copy-start.2
  30.8 8.5 %convolution_convert_fusion = bf16[1024,256]{1,0:T(8,128)(2,1)} fusion(bf16[5120,256]{1,0:T(8,128)(2,1)} %bitcast.22, bf16[1,1024,5120]{2,1,0:T(8,128)(2,1)} %param.7), kind=kOutput, calls=%fused_computation | convolution fusion | flops 2684616704 | bytes 13631488 | tf_op jit(solution)/shard_map/dot_general | solution.py:412
  39.4 0.0 copy-start
  39.4 0.0 copy-start.1
  39.4 0.0 all-gather.2.cloned.1.call-update
  40.1 0.0 copy-done.3
  40.1 0.6 fusion
  40.7 0.7 pad_add_fusion.lens_ref
  41.5 0.0 copy-done.2
  41.5 1.8 convolution_convert_fusion.1.rkv_ref
  43.3 41.1 %all-gather.2.cloned.1.call-done.kv_ref = bf16[4096,256]{1,0:T(8,128)(2,1)} async-done(((bf16[1024,256]{1,0:T(8,128)(2,1)}), bf16[4096,256]{1,0:T(8,128)(2,1)}) %all-gather.2.cloned.1.call-update) | async-done | bytes 2097168 | tf_op jit(solution)/shard_map/all_gather | solution.py:414
  84.4 0.0 copy-done
  84.4 0.0 copy-done.1
  84.4 28.9 %attend.1 = (bf16[128,1024]{1,0:T(8,128)(2,1)}, bf16[128,1024]{1,0:T(8,128)(2,1)}, f32[4096,256]{1,0:T(8,128)}, bf16[128,256]{1,0:T(8,128)(2,1)S(1)}) custom-call(s32[2]{0:T(128)S(1)} %pad_add_fusion.lens_ref, bf16[128,1024]{1,0:T(8,128)(2,1)S(1)} %bitcast.20, bf16[128,1024]{1,0:T(8,128)(2,1)S(1)} %bitcast.21, ...), custom_call_target="tpu_custom_call" | custom-call | tf_op jit(solution)/shard_map/attend/pallas_call | solution.py:383
  113.4 80.5 %finish.1 = (bf16[1024,256]{1,0:T(8,128)(2,1)S(1)}, f32[160,256]{1,0:T(8,128)S(1)}) custom-call(f32[4,1024,256]{2,1,0:T(8,128)} %bitcast.26, bf16[128,256]{1,0:T(8,128)(2,1)S(1)} %get-tuple-element.13.rgrad_ref, bf16[1024,5120]{1,0:T(8,128)(2,1)} %bitcast.24, bf16[128,5120]{1,0:T(8,128)(2,1)} %bitcast.25), custom_call_target="tpu_custom_call" | custom-call | tf_op jit(solution)/shard_map/finish/pallas_call | solution.py:246
  193.9 0.8 copy.14
  194.7 0.7 copy.15
Async XLA Ops:
  7.2 77.3 %all-gather.2.cloned.1.call-start = ((), (), s32[]{:S(2)}) async-start(), calls=%async_computation | async-start | bytes 2621440 | tf_op jit(solution)/shard_map/all_gather | solution.py:414
  30.8 9.3 %copy-start.3 = (s32[1,4]{1,0:T(1,128)S(1)}, s32[1,4]{1,0:T(1,128)}, u32[]{:S(2)}) copy-start(s32[1,4]{1,0:T(1,128)} %param.13) | copy-start | bytes 52
  30.8 10.6 %copy-start.2 = (bf16[32,160,256]{2,1,0:T(8,128)(2,1)S(1)}, bf16[32,160,256]{2,1,0:T(8,128)(2,1)}, u32[]{:S(2)}) copy-start(bf16[32,160,256]{2,1,0:T(8,128)(2,1)} %gather_weight.1) | copy-start | bytes 7864324
  39.4 45.1 %copy-start = (bf16[1,128,1024]{2,1,0:T(8,128)(2,1)S(1)}, bf16[1,128,1024]{2,1,0:T(8,128)(2,1)}, u32[]{:S(2)}) copy-start(bf16[1,128,1024]{2,1,0:T(8,128)(2,1)} %param.9) | copy-start | bytes 786436
  39.4 45.1 %copy-start.1 = (bf16[1,128,1024]{2,1,0:T(8,128)(2,1)S(1)}, bf16[1,128,1024]{2,1,0:T(8,128)(2,1)}, u32[]{:S(2)}) copy-start(bf16[1,128,1024]{2,1,0:T(8,128)(2,1)} %param.10) | copy-start | bytes 786436
Sparse Core Ops, SparseCore 0:
  39.5 44.8 all-gather.1
